TPU v7x, 256 devices: a whole 4x4x8 slice. The times are simulated.
256 devices in a mesh: query: 2 (over y_hi), wide: 128 (over z, y_lo, x, core).
Axes of the slice: x: 4, y: 4 (y_hi: 2, y_lo: 2; y = y_hi * 2 + y_lo), z: 8, core: 2. Of those that a mesh axis runs over, the one named last changes fastest.
Arguments:
- queries: bfloat16 [8192, 256], P(('query', 'wide')), may hold values from -3 to 3
- items: bfloat16 [131072, 256], P('wide'), may hold values from -24 to 24
- positive_ids: int32 [8192], P(('query', 'wide')), may hold values from 0 to 131071
Outputs:
- query_grad: float32 [8192, 256], P(('query', 'wide'))
- query_loss: float32 [8192], P(('query', 'wide'))
- item_grad: float32 [131072, 256], P('wide')
All inputs are finite; a program needn't handle non-finite values.
Results may differ from a plain program's by a relative error of at most 0.00085.
Values may be sent and summed in bfloat16 or wider, within the bound.
A program may use at most 64 MiB of HBM per device.

v0:
```python
import math

import jax
import jax.numpy as jnp
from jax import lax
from jax.sharding import PartitionSpec as P

logit_scale = 0.0625
logit_shift = -2.0


def local_pass(rows, wanted, panel, first_item):
    total_rows = rows.shape[0]
    width = rows.shape[1]
    block = math.gcd(total_rows, 512)
    count = total_rows // block
    rows_blocks = rows.reshape(count, block, width)
    wanted_blocks = wanted.reshape(count, block)
    column = first_item + jnp.arange(panel.shape[0], dtype=jnp.int32)

    def step(total, pair):
        part_rows, part_wanted = pair
        scores = (
            lax.dot_general(
                part_rows, panel, (((1,), (1,)), ((), ())), preferred_element_type=jnp.float32
            )
            * logit_scale
            + logit_shift
        )
        signs = jnp.where(column[None, :] == part_wanted[:, None], 1.0, -1.0).astype(jnp.float32)
        slopes = (-signs * jax.nn.sigmoid(-signs * scores)).astype(jnp.bfloat16)
        total = (
            total
            + lax.dot_general(
                slopes, part_rows, (((0,), (0,)), ((), ())), preferred_element_type=jnp.float32
            )
            * logit_scale
        )
        losses = jax.nn.softplus(-signs * scores)
        grads = jnp.dot(slopes, panel, preferred_element_type=jnp.float32) * logit_scale
        return (total, (grads, jnp.sum(losses, axis=1)))

    start_total = jnp.zeros((panel.shape[0], width), jnp.float32)
    item_total, outputs = lax.scan(step, start_total, (rows_blocks, wanted_blocks))
    return (item_total, outputs[0].reshape(total_rows, width), outputs[1].reshape(total_rows))


def body(queries, items, positive_ids):
    wide_count = lax.axis_size("wide")
    item_rows = items.shape[0]
    corpus = item_rows * wide_count
    first_item = lax.axis_index("wide") * item_rows
    rows = lax.all_gather(queries, "wide", axis=0, tiled=True)
    wanted = lax.all_gather(positive_ids, "wide", axis=0, tiled=True)
    item_part, grad_terms, loss_terms = local_pass(rows, wanted, items, first_item)
    item_grad = lax.psum(item_part, "query")
    query_grad, loss_sum = (
        lax.psum_scatter(grad_terms, "wide", scatter_dimension=0, tiled=True),
        lax.psum_scatter(loss_terms, "wide", scatter_dimension=0, tiled=True),
    )
    query_loss = loss_sum / corpus
    return (query_grad, query_loss, item_grad)


def solution(mesh):
    return jax.shard_map(
        body,
        mesh=mesh,
        in_specs=(P(("query", "wide"), None), P("wide", None), P(("query", "wide"))),
        out_specs=(P(("query", "wide"), None), P(("query", "wide")), P("wide", None)),
        check_vma=False,
    )
```

profile of v0, /device:TPU:18, one launch (start us, length us, event | category | flops | bytes accessed | tf_op | source)
XLA Modules:
  0.0 1246.0 jit_solution(11005686165480229292)
XLA Ops:
  8.0 1.4 fusion.12
  10.0 0.9 dynamic-update-slice
  10.9 550.6 %all-reduce = s32[4096]{0:T(1024)S(1)} all-reduce(s32[4096]{0:T(1024)S(1)} %dynamic-update-slice), channel_id=1, replica_groups=mesh['query'=2,'wide'=128] {'wide'}, use_global_device_ids=true, to_apply=%add | all-reduce | flops 4096 | bytes 32768
  561.5 55.4 %while.15 = (s32[]{:T(128)}, f32[1024,256]{1,0:T(8,128)S(1)}, f32[8,512,256]{2,1,0:T(8,128)}, f32[8,512]{1,0:T(8,128)S(1)}, s32[8,512]{1,0:T(8,128)S(1)}, /*inde...) while((s32[]{:T(128)}, f32[1024,256]{1,0:T(8,128)S(1)}, ...), condition=%wide.region_2.3_spmd.clone, body=%wide.region_0.2_spmd.clone.sunk | while | flops 821428736 | bytes 12615851 | solution.py:44
  561.5 3.0 fusion.24
  564.6 2.2 fusion.25
  566.8 1.6 fusion.26
  568.4 3.0 fusion.24
  571.5 2.2 fusion.25
  573.7 1.6 fusion.26
  575.4 3.0 fusion.24
  578.4 2.2 fusion.25
  580.7 1.6 fusion.26
  582.3 3.0 fusion.24
  585.4 2.2 fusion.25
  587.6 1.6 fusion.26
  589.2 3.0 fusion.24
  592.3 2.2 fusion.25
  594.5 1.6 fusion.26
  596.2 3.0 fusion.24
  599.2 2.2 fusion.25
  601.5 1.6 fusion.26
  603.1 3.0 fusion.24
  606.2 2.2 fusion.25
  608.4 1.6 fusion.26
  610.0 3.0 fusion.24
  613.1 2.2 fusion.25
  615.3 1.6 fusion.26
  616.9 1.0 copy-done
  619.2 549.2 %all-reduce.1 = f32[4096]{0:T(1024)S(1)} all-reduce(f32[4096]{0:T(1024)S(1)} %bitcast.36), channel_id=3, replica_groups=mesh['query'=2,'wide'=128] {'wide'}, use_global_device_ids=true, to_apply=%region_4.5.clone | all-reduce | flops 4096 | bytes 32768
  1169.0 68.2 %reduce-scatter.2.cloned.1.call-done = f32[32,256]{1,0:T(8,128)} async-done(((f32[4096,256]{1,0:T(8,128)}), f32[32,256]{1,0:T(8,128)}) %reduce-scatter.2.cloned.1.call-update) | async-done | bytes 32784 | tf_op jit(solution)/shard_map/reduce_scatter | solution.py:58
  1237.2 2.3 copy.23
  (56 shorter events, 2.7 us)
Async XLA Ops:
  7.2 554.3 %all-gather.2.cloned.1.call-start = ((), (), s32[]{:S(2)}) async-start(), calls=%async_computation.1 | async-start | bytes 2113536 | tf_op jit(solution)/shard_map/all_gather | solution.py:53
  7.9 1161.1 %all-reduce.4.cloned.1.call-start = ((), (), s32[]{:S(2)}) async-start(), calls=%async_computation.3 | async-start | bytes 2097152 | tf_op jit(solution)/shard_map/psum | solution.py:56
  564.6 2.2 copy-start.1
  571.5 2.2 copy-start.1
  578.4 2.2 copy-start.1
  585.4 2.2 copy-start.1
  592.3 2.2 copy-start.1
  599.2 2.2 copy-start.1
  606.1 2.2 copy-start.1
  613.0 2.2 copy-start.1
  616.9 1.0 copy-start
  617.9 619.3 %reduce-scatter.2.cloned.1.call-start = ((), (), s32[]{:S(2)}) async-start(), calls=%async_computation.2 | async-start | bytes 4227072 | tf_op jit(solution)/shard_map/reduce_scatter | solution.py:58
Sparse Core Ops, SparseCore 0:
  9.9 215.4 all-gather.1
  618.0 51.4 all-reduce.3
  672.7 564.4 reduce-scatter.1
where the time goes:
time: 1250 us
  blocking collectives  1100 us (88%)
  waiting for transfers between devices  69.6 us (6%)
  matrix products  54.5 us (4%)
  between operations  15 us (1%)
    unnamed x2, blocking collectives  1100 us
    reduce_scatter x1, waiting for transfers between devices, body(): lax.psum_scatter(grad_terms, 'wide', scatter_dimension=0, tiled=True)  68.2 us
  transfers between devices with their start and end apart: 3, of which 1 were waited for; matrix products, arithmetic and copies ran while one was open for 0% of the time, Pallas kernels for 0%

commit v1 on v0

v1 whole, which is shorter than its diff:
```python
import functools

import jax
import jax.numpy as jnp
from jax import lax
from jax.experimental import pallas as pl
from jax.experimental.pallas import tpu as pltpu
from jax.sharding import PartitionSpec as P

MESH = pl.DeviceIdType.MESH
logit_scale = 0.0625
logit_shift = -2.0
log2e = 1.4426950408889634

NZ, NY, NX, NC = 8, 2, 4, 2
BLOCK = 32
ROWS = NZ * NY * BLOCK
TALL = ROWS + 8
ITEMS = 1024
E = 256
OFFSETS = (0, 0, 1, 1, 3, 3, 2, 2)
ORDER = (0, 1, 0, 1, 1, 0, 1, 0)


def pick(step, table):
    total = 0
    for k, value in enumerate(table):
        if value:
            total = total + value * jnp.where(step == k, 1, 0)
    return total


def compute_tile(q, ids, panel, first_item, grad_total):
    z = lax.dot_general(q, panel, (((1,), (1,)), ((), ())), preferred_element_type=jnp.float32)
    wanted = jnp.concatenate(
        [jnp.broadcast_to(ids[:, j : j + 1], (8, 128)) for j in range(ROWS // 8)], axis=0
    )
    place = wanted - first_item - lax.broadcasted_iota(jnp.int32, (ROWS, 128), 1)
    slopes = []
    product, relus = None, None
    for c in range(ITEMS // 128):
        scores = z[:, c * 128 : (c + 1) * 128] + logit_shift
        hit = place == c * 128
        v = jnp.where(hit, -scores, scores)
        e = jnp.exp2(jnp.abs(v) * (-log2e))
        u = 1.0 + e
        r = 1.0 / u
        g = jnp.where(v >= 0, r, e * r)
        slopes.append(jnp.where(hit, -g, g).astype(jnp.bfloat16))
        relu = jnp.maximum(v, 0.0)
        product = e if product is None else product * u + e
        relus = relu if relus is None else relus + relu
    slope = jnp.concatenate(slopes, axis=1)
    grads = jnp.dot(slope, panel, preferred_element_type=jnp.float32)
    grad_total[...] += lax.dot_general(
        q, slope, (((0,), (0,)), ((), ())), preferred_element_type=jnp.float32
    )
    whole = 1.0 + product
    losses = relus + jnp.log(whole) + (product - (whole - 1.0)) / whole
    return grads, losses


def kernel(
    q_ref, ids_ref, items_ref, qgrad_ref, loss_ref, igrad_ref,
    qbuf, idz, idy, idm, tiles, sib_recv, x_recv, z_send, z_recv, z_sum, y_send, y_recv,
    ig_total, ig_send, ig_recv,
    gz_s, gz_r, iz_s, iz_r, gy_s, gy_r, iy_s, iy_r, gx_s, gx_r, ix_s, ix_r, gc_s, gc_r, ic_s, ic_r,
    tc_s, tc_r, tx_s, tx_r, tz_s, tz_r, ty_s, ty_r, ig_s, ig_r,
):
    hi = lax.axis_index("query")
    w = lax.axis_index("wide")
    core, x, lo, z = w % 2, (w // 2) % 4, (w // 8) % 2, w // 16

    def at(dz=0, dy=0, dx=0, dc=0, dh=0):
        zz, yy, xx, cc, hh = (z + dz) % NZ, (lo + dy) % NY, (x + dx) % NX, (core + dc) % NC, (hi + dh) % 2
        return (hh, ((zz * NY + yy) * NX + xx) * NC + cc)

    def copy(src, dst, send, recv, to):
        return pltpu.make_async_remote_copy(
            src_ref=src, dst_ref=dst, send_sem=send, recv_sem=recv, device_id=to, device_id_type=MESH
        )

    mine = pl.ds(pl.multiple_of(lo * (NZ * BLOCK) + z * BLOCK, BLOCK), BLOCK)
    qbuf[x, core, mine] = (q_ref[...].astype(jnp.float32) * logit_scale).astype(jnp.bfloat16)
    lane = lax.broadcasted_iota(jnp.int32, (8, 128), 1)
    sub = lax.broadcasted_iota(jnp.int32, (8, 128), 0)
    padded = jnp.concatenate([ids_ref[...], jnp.zeros((1, 96), jnp.int32)], axis=1)
    wide_ids = jnp.broadcast_to(padded, (8, 128))
    own_ids = jnp.zeros((8, 128), jnp.int32)
    for k in range(4):
        part = jnp.sum(jnp.where(lane == sub + k * 8, wide_ids, 0), axis=1, keepdims=True)
        own_ids = jnp.where(lane % 4 == k, jnp.broadcast_to(part, (8, 128)), own_ids)
    idz[z] = own_ids

    barrier = pltpu.get_barrier_semaphore()
    peers = [at(dz=k) for k in range(1, NZ)] + [at(dx=k) for k in range(1, NX)]
    peers += [at(dy=1), at(dc=1), at(dh=1)]
    for peer in peers:
        pl.semaphore_signal(barrier, inc=1, device_id=peer, device_id_type=MESH)
    pl.semaphore_wait(barrier, len(peers))

    def gz(k):
        return copy(qbuf.at[x, core, mine], qbuf.at[x, core, mine], gz_s.at[k], gz_r.at[k], at(dz=k))

    def iz(k):
        return copy(idz.at[z], idz.at[z], iz_s.at[k], iz_r.at[k], at(dz=k))

    for k in (4, 3, 5, 2, 6, 1, 7):
        iz(k).start()
        gz(k).start()
    ig_total[...] = jnp.zeros_like(ig_total)
    for k in range(1, NZ):
        iz(k).wait_recv()
    half_ids = jnp.zeros((8, 128), jnp.int32)
    for k in range(NZ):
        half_ids = jnp.where(lane // 4 == lo * NZ + k, idz[k], half_ids)
    idy[0] = half_ids
    iy = copy(idy.at[0], idy.at[1], iy_s, iy_r, at(dy=1))
    iy.start()
    for k in range(1, NZ):
        gz(k).wait_recv()

    half = pl.ds(pl.multiple_of(lo * (NZ * BLOCK), NZ * BLOCK), NZ * BLOCK)
    gy = copy(qbuf.at[x, core, half], qbuf.at[x, core, half], gy_s, gy_r, at(dy=1))
    gy.start()
    iy.wait_recv()
    idm[x, core] = half_ids + idy[1]

    def gx(k):
        return copy(qbuf.at[x, core], qbuf.at[x, core], gx_s.at[k], gx_r.at[k], at(dx=k))

    def ix(k):
        return copy(idm.at[x, core], idm.at[x, core], ix_s.at[k], ix_r.at[k], at(dx=k))

    def gc(k):
        xx = (x + NX - k) % NX
        return copy(qbuf.at[xx, core], qbuf.at[xx, core], gc_s.at[k], gc_r.at[k], at(dc=1))

    def ic(k):
        xx = (x + NX - k) % NX
        return copy(idm.at[xx, core], idm.at[xx, core], ic_s.at[k], ic_r.at[k], at(dc=1))

    for k in (1, 3, 2):
        ix(k).start()
    ic(0).start()
    gy.wait_recv()
    for k in (1, 3):
        gx(k).start()
    gc(0).start()

    def arrived(k):
        ix(k).wait_recv()
        gx(k).wait_recv()
        ic(k).start()
        gc(k).start()

    def from_sib(k):
        ic(k).wait_recv()
        gc(k).wait_recv()

    def tc(d):
        return copy(tiles.at[NX + d], sib_recv.at[d], tc_s.at[d], tc_r.at[d], at(dc=1))

    def tx(d):
        return copy(tiles.at[d], x_recv.at[d - 1], tx_s.at[d - 1], tx_r.at[d - 1], at(dx=d))

    def joined(d):
        tc(d).wait_recv()
        tiles[d] = tiles[d] + sib_recv[d]
        tx(d).start()

    def step(k, _):
        @pl.when(k == 1)
        def _():
            gx(2).start()
            from_sib(0)

        @pl.when(k == 2)
        def _():
            arrived(3)

        @pl.when(k == 3)
        def _():
            arrived(1)
            from_sib(3)

        @pl.when(k == 4)
        def _():
            from_sib(1)

        @pl.when(k == 5)
        def _():
            arrived(2)
            joined(1)

        @pl.when(k == 6)
        def _():
            from_sib(2)
            joined(3)

        off = pick(k, OFFSETS)
        other = pick(k, ORDER)
        xx, cc = (x + off) % NX, (core + other) % NC
        grads, losses = compute_tile(
            qbuf[xx, cc], idm[xx, cc], items_ref[...], (w * ITEMS), ig_total
        )
        slot = other * NX + off
        tiles[slot, 0:ROWS] = grads
        sums = [
            jnp.sum(losses[b * 128 : (b + 1) * 128].T, axis=0, keepdims=True) for b in range(ROWS // 128)
        ]
        block = jnp.concatenate(sums + [jnp.zeros((8 - len(sums), 128), jnp.float32)], axis=0)
        tiles[slot, ROWS:TALL] = jnp.concatenate([block, jnp.zeros((8, 128), jnp.float32)], axis=1)

        @pl.when(other == 1)
        def _():
            tc(off).start()

        return 0

    lax.fori_loop(0, len(ORDER), step, 0)

    joined(2)

    def ig(k):
        part = pl.ds(k * 256, 256)
        return copy(ig_send.at[part], ig_recv.at[part], ig_s.at[k], ig_r.at[k], at(dh=1))

    for k in range(ITEMS // 256):
        ig_send[k * 256 : (k + 1) * 256] = ig_total[:, k * 256 : (k + 1) * 256].T
        ig(k).start()

    tc(0).wait_recv()
    for d in range(1, NX):
        tx(d).wait_recv()

    def column_sum(rows):
        total = tiles[0, rows] + sib_recv[0, rows]
        for d in range(NX - 1):
            total = total + x_recv[d, rows]
        return total

    loss_block = column_sum(pl.ds(ROWS, 8))

    def fill(k, _):
        for yy in range(NY):
            rows = pl.ds(pl.multiple_of(yy * (NZ * BLOCK) + k * BLOCK, BLOCK), BLOCK)
            z_send[k, yy * BLOCK : (yy + 1) * BLOCK] = column_sum(rows)
        z_send[k, NY * BLOCK :] = loss_block
        return 0

    def tz(k):
        return copy(z_send.at[(z + k) % NZ], z_recv.at[k - 1], tz_s.at[k - 1], tz_r.at[k - 1], at(dz=k))

    lax.fori_loop(0, NZ, fill, 0)
    for k in (4, 3, 5, 2, 6, 1, 7):
        tz(k).start()
    for k in range(1, NZ):
        tz(k).wait_recv()
    total = z_send[z]
    for k in range(NZ - 1):
        total = total + z_recv[k]
    z_sum[...] = total
    other_rows = pl.ds(pl.multiple_of((1 - lo) * BLOCK, BLOCK), BLOCK)
    own_rows = pl.ds(pl.multiple_of(lo * BLOCK, BLOCK), BLOCK)
    y_send[0:BLOCK] = z_sum[other_rows]
    y_send[BLOCK:] = z_sum[NY * BLOCK :]
    ty = copy(y_send, y_recv, ty_s, ty_r, at(dy=1))
    ty.start()
    ty.wait_recv()
    qgrad_ref[...] = (z_sum[own_rows] + y_recv[0:BLOCK]) * logit_scale
    y_recv[BLOCK:] = z_sum[NY * BLOCK :] + y_recv[BLOCK:]
    line = jnp.where(sub == lo * 2 + z // 4, y_recv[BLOCK:, 0:128], 0.0)
    line = jnp.broadcast_to(jnp.sum(line, axis=0, keepdims=True), (8, 128))
    line = pltpu.roll(line, (128 - (z % 4) * BLOCK) % 128, 1)
    loss_ref[...] = line[0:1, 0:BLOCK] * (1.0 / (ITEMS * NZ * NY * NX * NC))

    for k in range(ITEMS // 256):
        part = slice(k * 256, (k + 1) * 256)
        ig(k).wait_recv()
        igrad_ref[part] = ig_send[part] + ig_recv[part]

    for k in range(1, NZ):
        iz(k).wait_send()
        gz(k).wait_send()
        tz(k).wait_send()
    iy.wait_send()
    gy.wait_send()
    ty.wait_send()
    for k in range(1, NX):
        ix(k).wait_send()
        gx(k).wait_send()
        tx(k).wait_send()
    for k in range(NX):
        ic(k).wait_send()
        gc(k).wait_send()
        tc(k).wait_send()
        ig(k).wait_send()


def body(queries, items, positive_ids):
    dma = pltpu.SemaphoreType.DMA
    vmem = pl.BlockSpec(memory_space=pltpu.VMEM)
    f32, bf16, i32 = jnp.float32, jnp.bfloat16, jnp.int32
    qgrad, loss, igrad = pl.pallas_call(
        kernel,
        out_shape=(
            jax.ShapeDtypeStruct((BLOCK, E), f32),
            jax.ShapeDtypeStruct((1, BLOCK), f32),
            jax.ShapeDtypeStruct((ITEMS, E), f32),
        ),
        in_specs=[vmem] * 3,
        out_specs=[vmem] * 3,
        scratch_shapes=[
            pltpu.VMEM((NX, NC, ROWS, E), bf16),
            pltpu.VMEM((NZ, 8, 128), i32),
            pltpu.VMEM((2, 8, 128), i32),
            pltpu.VMEM((NX, NC, 8, 128), i32),
            pltpu.VMEM((2 * NX, TALL, E), f32),
            pltpu.VMEM((NX, TALL, E), f32),
            pltpu.VMEM((NX - 1, TALL, E), f32),
            pltpu.VMEM((NZ, NY * BLOCK + 8, E), f32),
            pltpu.VMEM((NZ - 1, NY * BLOCK + 8, E), f32),
            pltpu.VMEM((NY * BLOCK + 8, E), f32),
            pltpu.VMEM((BLOCK + 8, E), f32),
            pltpu.VMEM((BLOCK + 8, E), f32),
            pltpu.VMEM((E, ITEMS), f32),
            pltpu.VMEM((ITEMS, E), f32),
            pltpu.VMEM((ITEMS, E), f32),
            dma((NZ,)), dma((NZ,)), dma((NZ,)), dma((NZ,)),
            dma, dma, dma, dma,
            dma((NX,)), dma((NX,)), dma((NX,)), dma((NX,)),
            dma((NX,)), dma((NX,)), dma((NX,)), dma((NX,)),
            dma((NX,)), dma((NX,)),
            dma((NX - 1,)), dma((NX - 1,)),
            dma((NZ - 1,)), dma((NZ - 1,)),
            dma, dma,
            dma((ITEMS // 256,)), dma((ITEMS // 256,)),
        ],
        compiler_params=pltpu.CompilerParams(
            collective_id=0, has_side_effects=True, vmem_limit_bytes=60 * 2**20
        ),
        cost_estimate=pl.CostEstimate(
            flops=6 * NX * NC * ROWS * ITEMS * E, bytes_accessed=4 * 2**20, transcendentals=2 * NX * NC * ROWS * ITEMS
        ),
    )(queries, positive_ids.reshape(1, BLOCK), items)
    return qgrad, loss.reshape(BLOCK), igrad


def solution(mesh):
    return jax.shard_map(
        body,
        mesh=mesh,
        in_specs=(P(("query", "wide"), None), P("wide", None), P(("query", "wide"))),
        out_specs=(P(("query", "wide"), None), P(("query", "wide")), P("wide", None)),
        check_vma=False,
    )
```

time: 1250 us -> 85.4 us (0.07)
  blocking collectives: 1100 us -> 0 us
  Pallas kernels: 0 us -> 80 us
  waiting for transfers between devices: 69.6 us -> 0 us
  matrix products: 54.5 us -> 0 us
  between operations: 15 us -> 0.65 us
    unnamed x2 -> x0, blocking collectives: 1100 us -> none
    pallas_call x0 -> x1, Pallas kernels: none -> 80 us  [body(): pl.pallas_call(kernel, out_shape=(jax.ShapeDtypeStruct((BLOCK, E), f32),...]
    reduce_scatter x1 -> x0, waiting for transfers between devices: 68.2 us -> none  [body(): lax.psum_scatter(grad_terms, 'wide', scatter_dimension=0, tiled=True)]
    dot_general x24 -> x0, matrix products: 54.5 us -> none  [the longest x8 24 us: step(): lax.dot_general(part_rows, panel, (((1,), (1,)), ((), ())), preferred_ele...]
  transfers between devices with their start and end apart: 3 -> 0, of which waited for: 1 -> 0; matrix products, arithmetic and copies ran while one was open for 0% -> 0% of each run, Pallas kernels for 0% -> 0%
where the time goes in v1:
time: 85.4 us; the launch traced here: 84.8 us
  Pallas kernels  80 us (94%)
  local copies, waits for them, and re-layouts  4.15 us (5%)
    pallas_call x1, Pallas kernels, body(): pl.pallas_call(kernel, out_shape=(jax.ShapeDtypeStruct((BLOCK, E), f32),...  80 us
    unnamed x5, local copies, waits for them, and re-layouts  4.15 us

profile of v1, /device:TPU:18, one launch (start us, length us, event | category | flops | bytes accessed | tf_op | source)
XLA Modules:
  0.0 84.8 jit_solution(16031738763872311)
XLA Ops:
  0.6 80.0 %shard_map.58 = (f32[32,256]{1,0:T(8,128)}, f32[1,32]{1,0:T(1,128)}, f32[1024,256]{1,0:T(8,128)}) custom-call(bf16[32,256]{1,0:T(8,128)(2,1)} %q_ref.1, s32[1,32]{1,0:T(1,128)} %bitcast.2, bf16[1024,256]{1,0:T(8,128)(2,1)} %items_ref.1), custom_call_target="tpu_custom_call" | custom-call | flops 6442450944 | bytes 4194304 | tf_op jit(solution)/shard_map/pallas_call | solution.py:305
  80.6 0.0 copy-start
  80.6 1.4 %copy.9 = f32[32,256]{1,0:T(8,128)} copy(f32[32,256]{1,0:T(8,128)} %get-tuple-element.12) | data formatting | bytes 65536
  82.0 0.0 copy-done
  82.0 0.5 copy.10
  82.5 2.3 %copy.11 = f32[1024,256]{1,0:T(8,128)} copy(f32[1024,256]{1,0:T(8,128)} %get-tuple-element.14) | data formatting | bytes 2097152
Async XLA Ops:
  80.6 1.4 %copy-start = (f32[1,32]{1,0:T(1,128)S(1)}, f32[1,32]{1,0:T(1,128)}, u32[]{:S(2)}) copy-start(f32[1,32]{1,0:T(1,128)} %get-tuple-element.7) | copy-start | bytes 388

commit v2 on v1

v2 whole, which is shorter than its diff:
```python
import jax
import jax.numpy as jnp
from jax import lax
from jax.experimental import pallas as pl
from jax.experimental.pallas import tpu as pltpu
from jax.sharding import PartitionSpec as P

MESH = pl.DeviceIdType.MESH
logit_scale = 0.0625
logit_shift = -2.0
log2e = 1.4426950408889634

NZ, NY, NX, NC = 8, 2, 4, 2
BLOCK = 32
COL = NZ * BLOCK
QCOL = COL + 16
TCOL = COL + 8
ZROWS = BLOCK + 8
ITEMS = 1024
E = 256
OFFSETS = (0, 1, 3, 2, 1, 3, 2, 0)


def pick(step, table):
    total = 0
    for k, value in enumerate(table):
        if value:
            total = total + value * jnp.where(step == k, 1, 0)
    return total


def compute_tile(q, ids, panel, first_item, grad_total):
    rows = NC * COL
    z = lax.dot_general(q, panel, (((1,), (1,)), ((), ())), preferred_element_type=jnp.float32)
    wanted = jnp.concatenate(
        [jnp.broadcast_to(ids[:, j : j + 1], (8, 128)) for j in range(rows // 8)], axis=0
    )
    place = wanted - first_item - lax.broadcasted_iota(jnp.int32, (rows, 128), 1)
    slopes = []
    product, relus = None, None
    for c in range(ITEMS // 128):
        scores = z[:, c * 128 : (c + 1) * 128] + logit_shift
        hit = place == c * 128
        v = jnp.where(hit, -scores, scores)
        e = jnp.exp2(jnp.abs(v) * (-log2e))
        u = 1.0 + e
        r = 1.0 / u
        g = jnp.where(v >= 0, r, e * r)
        slopes.append(jnp.where(hit, -g, g).astype(jnp.bfloat16))
        relu = jnp.maximum(v, 0.0)
        product = e if product is None else product * u + e
        relus = relu if relus is None else relus + relu
    slope = jnp.concatenate(slopes, axis=1)
    grads = jnp.dot(slope, panel, preferred_element_type=jnp.float32)
    grad_total[...] += lax.dot_general(
        slope, q, (((0,), (0,)), ((), ())), preferred_element_type=jnp.float32
    )
    whole = 1.0 + product
    losses = relus + jnp.log(whole) + (product - (whole - 1.0)) / whole
    return grads, losses


def kernel(
    q_ref, ids_ref, items_ref, qgrad_ref, loss_ref, ig_own, ig_other,
    qbuf, idz, tiles, sib_recv, x_recv, z_send, z_recv, y_send, y_recv, ig_total,
    gz_s, gz_r, iz_s, iz_r, gy_s, gy_r, gx_s, gx_r, ga_s, ga_r, gb_s, gb_r,
    tc_s, tc_r, tx_s, tx_r, tz_s, tz_r, ty_s, ty_r, ig_s, ig_r, out_s,
):
    hi = lax.axis_index("query")
    w = lax.axis_index("wide")
    core, x, lo, z = w % 2, (w // 2) % 4, (w // 8) % 2, w // 16

    def at(dz=0, dy=0, dx=0, dc=0, dh=0):
        zz, yy, xx, cc, hh = (z + dz) % NZ, (lo + dy) % NY, (x + dx) % NX, (core + dc) % NC, (hi + dh) % 2
        return (hh, ((zz * NY + yy) * NX + xx) * NC + cc)

    def copy(src, dst, send, recv, to):
        return pltpu.make_async_remote_copy(
            src_ref=src, dst_ref=dst, send_sem=send, recv_sem=recv, device_id=to, device_id_type=MESH
        )

    barrier = pltpu.get_barrier_semaphore()
    peers = [at(dz=k) for k in (4, 3, 5, 2, 6, 1, 7)] + [at(dx=k) for k in range(1, NX)]
    peers += [at(dy=1), at(dc=1), at(dh=1)]
    for peer in peers:
        pl.semaphore_signal(barrier, inc=1, device_id=peer, device_id_type=MESH)

    mine = pl.ds(pl.multiple_of(z * BLOCK, BLOCK), BLOCK)
    qbuf[x, lo, core, mine] = (q_ref[...].astype(jnp.float32) * logit_scale).astype(jnp.bfloat16)
    lane = lax.broadcasted_iota(jnp.int32, (8, 128), 1)
    sub = lax.broadcasted_iota(jnp.int32, (8, 128), 0)
    padded = jnp.concatenate([ids_ref[...], jnp.zeros((1, 96), jnp.int32)], axis=1)
    wide_ids = jnp.broadcast_to(padded, (8, 128))
    own_ids = jnp.zeros((8, 128), jnp.int32)
    for k in range(4):
        part = jnp.sum(jnp.where(lane == sub + k * 8, wide_ids, 0), axis=1, keepdims=True)
        own_ids = jnp.where(lane % 4 == k, jnp.broadcast_to(part, (8, 128)), own_ids)
    idz[z] = own_ids
    pl.semaphore_wait(barrier, len(peers))

    def gz(k):
        here = qbuf.at[x, lo, core, mine]
        return copy(here, here, gz_s.at[k], gz_r.at[k], at(dz=k))

    def iz(k):
        return copy(idz.at[z], idz.at[z], iz_s.at[k], iz_r.at[k], at(dz=k))

    for k in (4, 3, 5, 2, 6, 1, 7):
        iz(k).start()
        gz(k).start()
    ig_total[...] = jnp.zeros_like(ig_total)
    for k in range(1, NZ):
        iz(k).wait_recv()
    col_ids = jnp.zeros((8, 128), jnp.int32)
    for k in range(NZ):
        col_ids = jnp.where(lane // 4 == core * NZ + k, idz[k], col_ids)
    digits = [col_ids % 256, (col_ids // 256) % 256, col_ids // 65536, jnp.zeros_like(col_ids)]
    digits = [d.astype(jnp.float32) for d in digits]
    qbuf[x, lo, core, COL:QCOL] = jnp.concatenate(
        [jnp.concatenate(digits[:2], axis=1), jnp.concatenate(digits[2:], axis=1)], axis=0
    ).astype(jnp.bfloat16)
    for k in range(1, NZ):
        gz(k).wait_recv()

    def gx(k):
        here = qbuf.at[x, lo, core]
        return copy(here, here, gx_s.at[k], gx_r.at[k], at(dx=k))

    def ga(k):
        here = qbuf.at[(x + NX - k) % NX, lo, core]
        return copy(here, here, ga_s.at[k], ga_r.at[k], at(dc=1))

    def gy(k):
        here = qbuf.at[(x + NX - k) % NX, lo, core]
        return copy(here, here, gy_s.at[k], gy_r.at[k], at(dy=1))

    def gb(k):
        here = qbuf.at[(x + NX - k) % NX, 1 - lo, core]
        return copy(here, here, gb_s.at[k], gb_r.at[k], at(dc=1))

    gx(1).start()
    gx(3).start()
    ga(0).start()
    gy(0).start()

    def arrived(k):
        gx(k).wait_recv()
        ga(k).start()
        gy(k).start()

    def crossed(k):
        gy(k).wait_recv()
        gb(k).start()

    def tc(h, d):
        return copy(tiles.at[1, h, d], sib_recv.at[h, d], tc_s.at[h, d], tc_r.at[h, d], at(dc=1))

    def tx(h, d):
        return copy(tiles.at[0, h, d], x_recv.at[h, d - 1], tx_s.at[h, d], tx_r.at[h, d], at(dx=d))

    def joined(h, d):
        tc(h, d).wait_recv()
        tiles[0, h, d] = tiles[0, h, d] + sib_recv[h, d]
        tx(h, d).start()

    def step(k, _):
        @pl.when(k == 0)
        def _():
            ga(0).wait_recv()
            gx(2).start()

        @pl.when(k == 1)
        def _():
            arrived(3)
            arrived(1)
            ga(3).wait_recv()

        @pl.when(k == 2)
        def _():
            arrived(2)
            crossed(0)
            ga(1).wait_recv()

        @pl.when(k == 3)
        def _():
            joined(0, 1)
            crossed(3)
            ga(2).wait_recv()

        @pl.when(k == 4)
        def _():
            joined(0, 3)
            crossed(1)
            gb(3).wait_recv()

        @pl.when(k == 5)
        def _():
            joined(0, 2)
            crossed(2)
            gb(1).wait_recv()

        @pl.when(k == 6)
        def _():
            joined(1, 1)
            gb(2).wait_recv()

        @pl.when(k == 7)
        def _():
            joined(1, 3)
            gb(0).wait_recv()

        off = pick(k, OFFSETS)
        h = k // NX
        xx, yy = (x + off) % NX, (lo + h) % NY
        q = jnp.concatenate([qbuf[xx, yy, cc, 0:COL] for cc in range(NC)], axis=0)
        coded = (qbuf[xx, yy, 0, COL:QCOL] + qbuf[xx, yy, 1, COL:QCOL]).astype(jnp.float32)
        ids = coded[0:8, 0:128] + coded[0:8, 128:] * 256.0 + coded[8:, 0:128] * 65536.0
        grads, losses = compute_tile(q, ids.astype(jnp.int32), items_ref[...], w * ITEMS, ig_total)
        for cc in range(NC):
            whose = (core + cc) % NC
            tiles[whose, h, off, 0:COL] = grads[cc * COL : (cc + 1) * COL]
            sums = [
                jnp.sum(losses[cc * COL + b * 128 : cc * COL + (b + 1) * 128].T, axis=0, keepdims=True)
                for b in range(COL // 128)
            ]
            block = jnp.concatenate(sums + [jnp.zeros((8 - len(sums), 128), jnp.float32)], axis=0)
            tiles[whose, h, off, COL:TCOL] = jnp.concatenate(
                [block, jnp.zeros((8, 128), jnp.float32)], axis=1
            )
        tc(h, off).start()
        return 0

    lax.fori_loop(0, len(OFFSETS), step, 0)

    def ig(k):
        part = pl.ds(k * 256, 256)
        return copy(ig_total.at[part], ig_other.at[part], ig_s.at[k], ig_r.at[k], at(dh=1))

    for k in range(ITEMS // 256):
        ig(k).start()
    keep = pltpu.make_async_copy(ig_total, ig_own, out_s)
    keep.start()
    joined(1, 2)

    def tz(h, k):
        return copy(
            z_send.at[h, (z + k) % NZ], z_recv.at[h, k - 1], tz_s.at[h, k - 1], tz_r.at[h, k - 1], at(dz=k)
        )

    def along_x(h):
        tc(h, 0).wait_recv()
        for d in (1, 3, 2):
            tx(h, d).wait_recv()

        def column_sum(rows):
            total = tiles[0, h, 0, rows] + sib_recv[h, 0, rows]
            for d in range(NX - 1):
                total = total + x_recv[h, d, rows]
            return total

        loss_block = column_sum(slice(COL, TCOL))
        for k in range(NZ):
            z_send[h, k, 0:BLOCK] = column_sum(slice(k * BLOCK, (k + 1) * BLOCK))
            z_send[h, k, BLOCK:] = loss_block
        for k in (4, 3, 5, 2, 6, 1, 7):
            tz(h, k).start()

    def along_z(h):
        for k in range(1, NZ):
            tz(h, k).wait_recv()
        total = z_send[h, z]
        for k in range(NZ - 1):
            total = total + z_recv[h, k]
        return total

    along_x(0)
    along_x(1)
    own_part = along_z(0)
    y_send[...] = along_z(1)
    ty = copy(y_send, y_recv, ty_s, ty_r, at(dy=1))
    ty.start()
    ty.wait_recv()
    total = own_part + y_recv[...]
    qgrad_ref[...] = total[0:BLOCK] * logit_scale
    line = jnp.where(sub == z // 4, total[BLOCK:, 0:128], 0.0)
    line = jnp.broadcast_to(jnp.sum(line, axis=0, keepdims=True), (8, 128))
    line = pltpu.roll(line, (128 - (z % 4) * BLOCK) % 128, 1)
    loss_ref[...] = line[0:1, 0:BLOCK] * (1.0 / (ITEMS * NZ * NY * NX * NC))

    keep.wait()
    for k in range(ITEMS // 256):
        ig(k).wait_recv()

    for k in range(1, NZ):
        iz(k).wait_send()
        gz(k).wait_send()
        for h in range(NY):
            tz(h, k).wait_send()
    ty.wait_send()
    for k in range(NX):
        if k:
            gx(k).wait_send()
        ga(k).wait_send()
        gy(k).wait_send()
        gb(k).wait_send()
        for h in range(NY):
            tc(h, k).wait_send()
            if k:
                tx(h, k).wait_send()
        ig(k).wait_send()


def finish(qgrad_in, loss_in, own, other, qgrad, loss, igrad):
    igrad[...] = own[...] + other[...]

    @pl.when(pl.program_id(0) == 0)
    def _():
        qgrad[...] = qgrad_in[...]
        loss[...] = loss_in[...]


def body(queries, items, positive_ids):
    dma = pltpu.SemaphoreType.DMA
    vmem = pl.BlockSpec(memory_space=pltpu.VMEM)
    anywhere = pl.BlockSpec(memory_space=pl.ANY)
    f32, bf16, i32 = jnp.float32, jnp.bfloat16, jnp.int32
    small = (jax.ShapeDtypeStruct((BLOCK, E), f32), jax.ShapeDtypeStruct((1, BLOCK), f32))
    large = jax.ShapeDtypeStruct((ITEMS, E), f32)
    qgrad, loss, own, other = pl.pallas_call(
        kernel,
        out_shape=small + (large, large),
        in_specs=[vmem] * 3,
        out_specs=[vmem] * 2 + [anywhere] * 2,
        scratch_shapes=[
            pltpu.VMEM((NX, NY, NC, QCOL, E), bf16),
            pltpu.VMEM((NZ, 8, 128), i32),
            pltpu.VMEM((NC, NY, NX, TCOL, E), f32),
            pltpu.VMEM((NY, NX, TCOL, E), f32),
            pltpu.VMEM((NY, NX - 1, TCOL, E), f32),
            pltpu.VMEM((NY, NZ, ZROWS, E), f32),
            pltpu.VMEM((NY, NZ - 1, ZROWS, E), f32),
            pltpu.VMEM((ZROWS, E), f32),
            pltpu.VMEM((ZROWS, E), f32),
            pltpu.VMEM((ITEMS, E), f32),
            dma((NZ,)), dma((NZ,)), dma((NZ,)), dma((NZ,)),
            dma((NX,)), dma((NX,)), dma((NX,)), dma((NX,)),
            dma((NX,)), dma((NX,)), dma((NX,)), dma((NX,)),
            dma((NY, NX)), dma((NY, NX)), dma((NY, NX)), dma((NY, NX)),
            dma((NY, NZ - 1)), dma((NY, NZ - 1)),
            dma, dma,
            dma((ITEMS // 256,)), dma((ITEMS // 256,)),
            dma,
        ],
        compiler_params=pltpu.CompilerParams(
            collective_id=0, has_side_effects=True, vmem_limit_bytes=56 * 2**20
        ),
    )(queries, positive_ids.reshape(1, BLOCK), items)
    parts = 4
    slab = pl.BlockSpec((ITEMS // parts, E), lambda i: (i, 0))
    whole = [pl.BlockSpec(s.shape, lambda i: (0, 0)) for s in small]
    qgrad, loss, igrad = pl.pallas_call(
        finish,
        grid=(parts,),
        out_shape=small + (large,),
        in_specs=whole + [slab, slab],
        out_specs=whole + [slab],
    )(qgrad, loss, own, other)
    return qgrad, loss.reshape(BLOCK), igrad


def solution(mesh):
    return jax.shard_map(
        body,
        mesh=mesh,
        in_specs=(P(("query", "wide"), None), P("wide", None), P(("query", "wide"))),
        out_specs=(P(("query", "wide"), None), P(("query", "wide")), P("wide", None)),
        check_vma=False,
    )
```

time: 85.4 us -> 71.3 us (0.83)
  Pallas kernels: 80 us -> 70.5 us
  local copies, waits for them, and re-layouts: 4.15 us -> 0 us
    pallas_call x1 -> x2, Pallas kernels: 80 us -> 70.5 us  [the longest x1 66.9 us: body(): pl.pallas_call(kernel, out_shape=small + (large, large), in_specs=[vmem]...]
    unnamed x5 -> x0, local copies, waits for them, and re-layouts: 4.15 us -> none
where the time goes in v2:
time: 71.3 us; the launch traced here: 71.2 us
  Pallas kernels  70.5 us (99%)
    pallas_call x1, Pallas kernels, body(): pl.pallas_call(kernel, out_shape=small + (large, large), in_specs=[vmem]...  66.9 us
    pallas_call x1, Pallas kernels, body(): pl.pallas_call(finish, grid=(parts,), out_shape=small + (large,), in_spec...  3.59 us

profile of v2, /device:TPU:18, one launch (start us, length us, event | category | flops | bytes accessed | tf_op | source)
XLA Modules:
  0.0 71.2 jit_solution(14546082817683334389)
XLA Ops:
  0.6 66.9 %shard_map.58 = (f32[32,256]{1,0:T(8,128)}, f32[1,32]{1,0:T(1,128)}, f32[1024,256]{1,0:T(8,128)}, f32[1024,256]{1,0:T(8,128)}) custom-call(bf16[32,256]{1,0:T(8,128)(2,1)} %q_ref.1, s32[1,32]{1,0:T(1,128)} %bitcast.2, bf16[1024,256]{1,0:T(8,128)(2,1)} %items_ref.1), custom_call_target="tpu_custom_call" | custom-call | tf_op jit(solution)/shard_map/pallas_call | solution.py:329
  67.6 3.6 %shard_map.59 = (f32[32,256]{1,0:T(8,128)}, f32[1,32]{1,0:T(1,128)}, f32[1024,256]{1,0:T(8,128)}) custom-call(f32[32,256]{1,0:T(8,128)} %get-tuple-element.10.qgrad_in, f32[1,32]{1,0:T(1,128)} %get-tuple-element.11.loss_in, f32[1024,256]{1,0:T(8,128)} %get-tuple-element.12.own, f32[1024,256]{1,0:T(8,128)} %get-tuple-element.13.other), custom_call_target="tpu_custom_call" | custom-call | tf_op jit(solution)/shard_map/pallas_call | solution.py:361

commit v3 on v2

--- a/solution.py
+++ b/solution.py
@@ -18,7 +18,9 @@
 ZROWS = BLOCK + 8
 ITEMS = 1024
 E = 256
-OFFSETS = (0, 1, 3, 2, 1, 3, 2, 0)
+OFFSETS = (0, 1, 3, 2, 1, 3)
+LAST = (2, 0)
+HALF = ITEMS // 2
 
 
 def pick(step, table):
@@ -38,7 +40,7 @@
     place = wanted - first_item - lax.broadcasted_iota(jnp.int32, (rows, 128), 1)
     slopes = []
     product, relus = None, None
-    for c in range(ITEMS // 128):
+    for c in range(panel.shape[0] // 128):
         scores = z[:, c * 128 : (c + 1) * 128] + logit_shift
         hit = place == c * 128
         v = jnp.where(hit, -scores, scores)
@@ -68,11 +70,19 @@
 ):
     hi = lax.axis_index("query")
     w = lax.axis_index("wide")
-    core, x, lo, z = w % 2, (w // 2) % 4, (w // 8) % 2, w // 16
+    core, x, lo, z = lax.rem(w, 2), lax.rem(w // 2, 4), lax.rem(w // 8, 2), w // 16
 
     def at(dz=0, dy=0, dx=0, dc=0, dh=0):
-        zz, yy, xx, cc, hh = (z + dz) % NZ, (lo + dy) % NY, (x + dx) % NX, (core + dc) % NC, (hi + dh) % 2
-        return (hh, ((zz * NY + yy) * NX + xx) * NC + cc)
+        to = w
+        if dz:
+            to = to + (lax.rem(z + dz, NZ) - z) * (NY * NX * NC)
+        if dy:
+            to = to + (1 - 2 * lo) * (NX * NC)
+        if dx:
+            to = to + (lax.rem(x + dx, NX) - x) * NC
+        if dc:
+            to = to + (1 - 2 * core)
+        return (1 - hi if dh else hi, to)
 
     def copy(src, dst, send, recv, to):
         return pltpu.make_async_remote_copy(
@@ -127,15 +137,15 @@
         return copy(here, here, gx_s.at[k], gx_r.at[k], at(dx=k))
 
     def ga(k):
-        here = qbuf.at[(x + NX - k) % NX, lo, core]
+        here = qbuf.at[lax.rem(x + NX - k, NX), lo, core]
         return copy(here, here, ga_s.at[k], ga_r.at[k], at(dc=1))
 
     def gy(k):
-        here = qbuf.at[(x + NX - k) % NX, lo, core]
+        here = qbuf.at[lax.rem(x + NX - k, NX), lo, core]
         return copy(here, here, gy_s.at[k], gy_r.at[k], at(dy=1))
 
     def gb(k):
-        here = qbuf.at[(x + NX - k) % NX, 1 - lo, core]
+        here = qbuf.at[lax.rem(x + NX - k, NX), 1 - lo, core]
         return copy(here, here, gb_s.at[k], gb_r.at[k], at(dc=1))
 
     gx(1).start()
@@ -155,13 +165,60 @@
     def tc(h, d):
         return copy(tiles.at[1, h, d], sib_recv.at[h, d], tc_s.at[h, d], tc_r.at[h, d], at(dc=1))
 
-    def tx(h, d):
-        return copy(tiles.at[0, h, d], x_recv.at[h, d - 1], tx_s.at[h, d], tx_r.at[h, d], at(dx=d))
+    def tx(h, d, s):
+        rows = slice(0, TCOL if s == 0 else COL)
+        return copy(
+            tiles.at[0, h, d, s, rows], x_recv.at[h, d - 1, s, rows],
+            tx_s.at[h, d, s], tx_r.at[h, d, s], at(dx=d),
+        )
 
     def joined(h, d):
         tc(h, d).wait_recv()
         tiles[0, h, d] = tiles[0, h, d] + sib_recv[h, d]
-        tx(h, d).start()
+        for s in range(2):
+            tx(h, d, s).start()
+
+    def tz(h, k, s):
+        rows = slice(0, ZROWS if s == 0 else BLOCK)
+        return copy(
+            z_send.at[h, s, lax.rem(z + k, NZ), rows], z_recv.at[h, s, k - 1, rows],
+            tz_s.at[h, s, k - 1], tz_r.at[h, s, k - 1], at(dz=k),
+        )
+
+    def along_x(h):
+        tc(h, 0).wait_recv()
+        for s in range(2):
+            for d in (1, 3, 2):
+                tx(h, d, s).wait_recv()
+
+            def column_sum(rows):
+                total = tiles[0, h, 0, s, rows] + sib_recv[h, 0, s, rows]
+                for d in range(NX - 1):
+                    total = total + x_recv[h, d, s, rows]
+                return total
+
+            for k in range(NZ):
+                z_send[h, s, k, 0:BLOCK] = column_sum(slice(k * BLOCK, (k + 1) * BLOCK))
+            if s == 0:
+                loss_block = column_sum(slice(COL, TCOL))
+                for k in range(NZ):
+                    z_send[h, s, k, BLOCK:] = loss_block
+            for k in (4, 3, 5, 2, 6, 1, 7):
+                tz(h, k, s).start()
+
+    def column(h, off):
+        xx, yy = lax.rem(x + off, NX), lax.rem(lo + h, NY)
+        q = jnp.concatenate([qbuf[xx, yy, cc, 0:COL] for cc in range(NC)], axis=0)
+        coded = (qbuf[xx, yy, 0, COL:QCOL] + qbuf[xx, yy, 1, COL:QCOL]).astype(jnp.float32)
+        ids = coded[0:8, 0:128] + coded[0:8, 128:] * 256.0 + coded[8:, 0:128] * 65536.0
+        return q, ids.astype(jnp.int32)
+
+    def loss_rows(losses, cc):
+        sums = [
+            jnp.sum(losses[cc * COL + b * 128 : cc * COL + (b + 1) * 128].T, axis=0, keepdims=True)
+            for b in range(COL // 128)
+        ]
+        return jnp.concatenate(sums + [jnp.zeros((8 - len(sums), 128), jnp.float32)], axis=0)
 
     def step(k, _):
         @pl.when(k == 0)
@@ -199,34 +256,16 @@
             crossed(2)
             gb(1).wait_recv()
 
-        @pl.when(k == 6)
-        def _():
-            joined(1, 1)
-            gb(2).wait_recv()
-
-        @pl.when(k == 7)
-        def _():
-            joined(1, 3)
-            gb(0).wait_recv()
-
         off = pick(k, OFFSETS)
         h = k // NX
-        xx, yy = (x + off) % NX, (lo + h) % NY
-        q = jnp.concatenate([qbuf[xx, yy, cc, 0:COL] for cc in range(NC)], axis=0)
-        coded = (qbuf[xx, yy, 0, COL:QCOL] + qbuf[xx, yy, 1, COL:QCOL]).astype(jnp.float32)
-        ids = coded[0:8, 0:128] + coded[0:8, 128:] * 256.0 + coded[8:, 0:128] * 65536.0
-        grads, losses = compute_tile(q, ids.astype(jnp.int32), items_ref[...], w * ITEMS, ig_total)
+        q, ids = column(h, off)
+        grads, losses = compute_tile(q, ids, items_ref[...], w * ITEMS, ig_total)
         for cc in range(NC):
-            whose = (core + cc) % NC
-            tiles[whose, h, off, 0:COL] = grads[cc * COL : (cc + 1) * COL]
-            sums = [
-                jnp.sum(losses[cc * COL + b * 128 : cc * COL + (b + 1) * 128].T, axis=0, keepdims=True)
-                for b in range(COL // 128)
-            ]
-            block = jnp.concatenate(sums + [jnp.zeros((8 - len(sums), 128), jnp.float32)], axis=0)
-            tiles[whose, h, off, COL:TCOL] = jnp.concatenate(
-                [block, jnp.zeros((8, 128), jnp.float32)], axis=1
-            )
+            whose = lax.rem(core + cc, NC)
+            for s in range(2):
+                tiles[whose, h, off, s, 0:COL] = grads[cc * COL : (cc + 1) * COL, s * 128 : (s + 1) * 128]
+            tiles[whose, h, off, 0, COL:TCOL] = loss_rows(losses, cc)
+            tiles[whose, h, off, 1, COL:TCOL] = jnp.zeros((8, 128), jnp.float32)
         tc(h, off).start()
         return 0
 
@@ -236,55 +275,85 @@
         part = pl.ds(k * 256, 256)
         return copy(ig_total.at[part], ig_other.at[part], ig_s.at[k], ig_r.at[k], at(dh=1))
 
-    for k in range(ITEMS // 256):
+    def late_step(k, _):
+        @pl.when(k == 0)
+        def _():
+            joined(1, 1)
+            gb(2).wait_recv()
+
+        @pl.when(k == 1)
+        def _():
+            joined(1, 3)
+            gb(0).wait_recv()
+
+        @pl.when(k == 2)
+        def _():
+            for part in range(HALF // 256):
+                ig(part).start()
+
+        @pl.when(k == 3)
+        def _():
+            along_x(0)
+
+        off = pick(k % len(LAST), LAST)
+        first = pl.multiple_of((k // len(LAST)) * HALF, HALF)
+        q, ids = column(1, off)
+        here = pl.ds(first, HALF)
+        grads, losses = compute_tile(q, ids, items_ref[here], w * ITEMS + first, ig_total.at[here])
+        for cc in range(NC):
+            whose = lax.rem(core + cc, NC)
+            part = grads[cc * COL : (cc + 1) * COL]
+            rows = loss_rows(losses, cc)
+
+            @pl.when(k < len(LAST))
+            def _():
+                for s in range(2):
+                    tiles[whose, 1, off, s, 0:COL] = part[:, s * 128 : (s + 1) * 128]
+                tiles[whose, 1, off, 0, COL:TCOL] = rows
+                tiles[whose, 1, off, 1, COL:TCOL] = jnp.zeros((8, 128), jnp.float32)
+
+            @pl.when(k >= len(LAST))
+            def _():
+                for s in range(2):
+                    tiles[whose, 1, off, s, 0:COL] += part[:, s * 128 : (s + 1) * 128]
+                tiles[whose, 1, off, 0, COL:TCOL] += rows
+
+        @pl.when(k >= len(LAST))
+        def _():
+            tc(1, off).start()
+
+        return 0
+
+    lax.fori_loop(0, 2 * len(LAST), late_step, 0)
+
+    for k in range(HALF // 256, ITEMS // 256):
         ig(k).start()
     keep = pltpu.make_async_copy(ig_total, ig_own, out_s)
     keep.start()
     joined(1, 2)
 
-    def tz(h, k):
-        return copy(
-            z_send.at[h, (z + k) % NZ], z_recv.at[h, k - 1], tz_s.at[h, k - 1], tz_r.at[h, k - 1], at(dz=k)
-        )
-
-    def along_x(h):
-        tc(h, 0).wait_recv()
-        for d in (1, 3, 2):
-            tx(h, d).wait_recv()
-
-        def column_sum(rows):
-            total = tiles[0, h, 0, rows] + sib_recv[h, 0, rows]
-            for d in range(NX - 1):
-                total = total + x_recv[h, d, rows]
-            return total
-
-        loss_block = column_sum(slice(COL, TCOL))
-        for k in range(NZ):
-            z_send[h, k, 0:BLOCK] = column_sum(slice(k * BLOCK, (k + 1) * BLOCK))
-            z_send[h, k, BLOCK:] = loss_block
-        for k in (4, 3, 5, 2, 6, 1, 7):
-            tz(h, k).start()
-
-    def along_z(h):
+    def along_z(h, s):
+        rows = slice(0, ZROWS if s == 0 else BLOCK)
         for k in range(1, NZ):
-            tz(h, k).wait_recv()
-        total = z_send[h, z]
+            tz(h, k, s).wait_recv()
+        total = z_send[h, s, z, rows]
         for k in range(NZ - 1):
-            total = total + z_recv[h, k]
+            total = total + z_recv[h, s, k, rows]
         return total
 
-    along_x(0)
     along_x(1)
-    own_part = along_z(0)
-    y_send[...] = along_z(1)
+    own_part = [along_z(0, s) for s in range(2)]
+    for s in range(2):
+        y_send[s * ZROWS : s * ZROWS + (ZROWS if s == 0 else BLOCK)] = along_z(1, s)
     ty = copy(y_send, y_recv, ty_s, ty_r, at(dy=1))
     ty.start()
     ty.wait_recv()
-    total = own_part + y_recv[...]
-    qgrad_ref[...] = total[0:BLOCK] * logit_scale
-    line = jnp.where(sub == z // 4, total[BLOCK:, 0:128], 0.0)
+    left = own_part[0] + y_recv[0:ZROWS]
+    qgrad_ref[:, 0:128] = left[0:BLOCK] * logit_scale
+    qgrad_ref[:, 128:] = (own_part[1] + y_recv[ZROWS:]) * logit_scale
+    line = jnp.where(sub == z // 4, left[BLOCK:], 0.0)
     line = jnp.broadcast_to(jnp.sum(line, axis=0, keepdims=True), (8, 128))
-    line = pltpu.roll(line, (128 - (z % 4) * BLOCK) % 128, 1)
+    line = pltpu.roll(line, lax.rem(128 - lax.rem(z, 4) * BLOCK, 128), 1)
     loss_ref[...] = line[0:1, 0:BLOCK] * (1.0 / (ITEMS * NZ * NY * NX * NC))
 
     keep.wait()
@@ -295,7 +364,8 @@
         iz(k).wait_send()
         gz(k).wait_send()
         for h in range(NY):
-            tz(h, k).wait_send()
+            for s in range(2):
+                tz(h, k, s).wait_send()
     ty.wait_send()
     for k in range(NX):
         if k:
@@ -306,7 +376,8 @@
         for h in range(NY):
             tc(h, k).wait_send()
             if k:
-                tx(h, k).wait_send()
+                for s in range(2):
+                    tx(h, k, s).wait_send()
         ig(k).wait_send()
 
 
@@ -334,19 +405,19 @@
         scratch_shapes=[
             pltpu.VMEM((NX, NY, NC, QCOL, E), bf16),
             pltpu.VMEM((NZ, 8, 128), i32),
-            pltpu.VMEM((NC, NY, NX, TCOL, E), f32),
-            pltpu.VMEM((NY, NX, TCOL, E), f32),
-            pltpu.VMEM((NY, NX - 1, TCOL, E), f32),
-            pltpu.VMEM((NY, NZ, ZROWS, E), f32),
-            pltpu.VMEM((NY, NZ - 1, ZROWS, E), f32),
-            pltpu.VMEM((ZROWS, E), f32),
-            pltpu.VMEM((ZROWS, E), f32),
+            pltpu.VMEM((NC, NY, NX, 2, TCOL, 128), f32),
+            pltpu.VMEM((NY, NX, 2, TCOL, 128), f32),
+            pltpu.VMEM((NY, NX - 1, 2, TCOL, 128), f32),
+            pltpu.VMEM((NY, 2, NZ, ZROWS, 128), f32),
+            pltpu.VMEM((NY, 2, NZ - 1, ZROWS, 128), f32),
+            pltpu.VMEM((ZROWS + BLOCK, 128), f32),
+            pltpu.VMEM((ZROWS + BLOCK, 128), f32),
             pltpu.VMEM((ITEMS, E), f32),
             dma((NZ,)), dma((NZ,)), dma((NZ,)), dma((NZ,)),
             dma((NX,)), dma((NX,)), dma((NX,)), dma((NX,)),
             dma((NX,)), dma((NX,)), dma((NX,)), dma((NX,)),
-            dma((NY, NX)), dma((NY, NX)), dma((NY, NX)), dma((NY, NX)),
-            dma((NY, NZ - 1)), dma((NY, NZ - 1)),
+            dma((NY, NX)), dma((NY, NX)), dma((NY, NX, 2)), dma((NY, NX, 2)),
+            dma((NY, 2, NZ - 1)), dma((NY, 2, NZ - 1)),
             dma, dma,
             dma((ITEMS // 256,)), dma((ITEMS // 256,)),
             dma,
@@ -355,7 +426,7 @@
             collective_id=0, has_side_effects=True, vmem_limit_bytes=56 * 2**20
         ),
     )(queries, positive_ids.reshape(1, BLOCK), items)
-    parts = 4
+    parts = 2
     slab = pl.BlockSpec((ITEMS // parts, E), lambda i: (i, 0))
     whole = [pl.BlockSpec(s.shape, lambda i: (0, 0)) for s in small]
     qgrad, loss, igrad = pl.pallas_call(

time: 71.3 us -> 67.1 us (0.941); the launches traced: 71.2 us -> 66 us
  Pallas kernels: 70.5 us -> 65.3 us
    pallas_call x1, Pallas kernels: 66.9 us -> 62.9 us  [body(): pl.pallas_call(kernel, out_shape=small + (large, large), in_specs=[vmem]...]
    pallas_call x1, Pallas kernels: 3.59 us -> 2.43 us  [body(): pl.pallas_call(finish, grid=(parts,), out_shape=small + (large,), in_spec...]
where the time goes in v3:
time: 67.1 us; the launch traced here: 66 us
  Pallas kernels  65.3 us (97%)
    pallas_call x1, Pallas kernels, body(): pl.pallas_call(kernel, out_shape=small + (large, large), in_specs=[vmem]...  62.9 us
    pallas_call x1, Pallas kernels, body(): pl.pallas_call(finish, grid=(parts,), out_shape=small + (large,), in_spec...  2.43 us

profile of v3, /device:TPU:18, one launch (start us, length us, event | category | flops | bytes accessed | tf_op | source)
XLA Modules:
  0.0 66.0 jit_solution(13214761326145710342)
XLA Ops:
  0.6 62.9 %shard_map.58 = (f32[32,256]{1,0:T(8,128)}, f32[1,32]{1,0:T(1,128)}, f32[1024,256]{1,0:T(8,128)}, f32[1024,256]{1,0:T(8,128)}) custom-call(bf16[32,256]{1,0:T(8,128)(2,1)} %q_ref.1, s32[1,32]{1,0:T(1,128)} %bitcast.2, bf16[1024,256]{1,0:T(8,128)(2,1)} %items_ref.1), custom_call_target="tpu_custom_call" | custom-call | tf_op jit(solution)/shard_map/pallas_call | solution.py:400
  63.5 2.4 %shard_map.59 = (f32[32,256]{1,0:T(8,128)}, f32[1,32]{1,0:T(1,128)}, f32[1024,256]{1,0:T(8,128)}) custom-call(f32[32,256]{1,0:T(8,128)} %get-tuple-element.10.qgrad_in, f32[1,32]{1,0:T(1,128)} %get-tuple-element.11.loss_in, f32[1024,256]{1,0:T(8,128)} %get-tuple-element.12.own, f32[1024,256]{1,0:T(8,128)} %get-tuple-element.13.other), custom_call_target="tpu_custom_call" | custom-call | tf_op jit(solution)/shard_map/pallas_call | solution.py:432

commit v4 on v3

--- a/solution.py
+++ b/solution.py
@@ -18,9 +18,9 @@
 ZROWS = BLOCK + 8
 ITEMS = 1024
 E = 256
-OFFSETS = (0, 1, 3, 2, 1, 3)
-LAST = (2, 0)
-HALF = ITEMS // 2
+OFFSETS = (0, 1, 3, 2, 1, 3, 2)
+LAST = (0,)
+PART = 256
 
 
 def pick(step, table):
@@ -32,10 +32,10 @@
 
 
 def compute_tile(q, ids, panel, first_item, grad_total):
-    rows = NC * COL
+    rows = q.shape[0]
     z = lax.dot_general(q, panel, (((1,), (1,)), ((), ())), preferred_element_type=jnp.float32)
     wanted = jnp.concatenate(
-        [jnp.broadcast_to(ids[:, j : j + 1], (8, 128)) for j in range(rows // 8)], axis=0
+        [jnp.broadcast_to(i[:, j : j + 1], (8, 128)) for i in ids for j in range(NC * COL // 8)], axis=0
     )
     place = wanted - first_item - lax.broadcasted_iota(jnp.int32, (rows, 128), 1)
     slopes = []
@@ -43,12 +43,13 @@
     for c in range(panel.shape[0] // 128):
         scores = z[:, c * 128 : (c + 1) * 128] + logit_shift
         hit = place == c * 128
-        v = jnp.where(hit, -scores, scores)
-        e = jnp.exp2(jnp.abs(v) * (-log2e))
+        sign = jnp.where(hit, -1.0, 1.0)
+        v = scores * sign
+        e = jnp.exp2(jnp.abs(scores) * (-log2e))
         u = 1.0 + e
         r = 1.0 / u
         g = jnp.where(v >= 0, r, e * r)
-        slopes.append(jnp.where(hit, -g, g).astype(jnp.bfloat16))
+        slopes.append((g * sign).astype(jnp.bfloat16))
         relu = jnp.maximum(v, 0.0)
         product = e if product is None else product * u + e
         relus = relu if relus is None else relus + relu
@@ -256,10 +257,15 @@
             crossed(2)
             gb(1).wait_recv()
 
+        @pl.when(k == 6)
+        def _():
+            joined(1, 1)
+            gb(2).wait_recv()
+
         off = pick(k, OFFSETS)
         h = k // NX
         q, ids = column(h, off)
-        grads, losses = compute_tile(q, ids, items_ref[...], w * ITEMS, ig_total)
+        grads, losses = compute_tile(q, [ids], items_ref[...], w * ITEMS, ig_total)
         for cc in range(NC):
             whose = lax.rem(core + cc, NC)
             for s in range(2):
@@ -275,62 +281,66 @@
         part = pl.ds(k * 256, 256)
         return copy(ig_total.at[part], ig_other.at[part], ig_s.at[k], ig_r.at[k], at(dh=1))
 
+    joined_at = ITEMS // PART - 1
+
     def late_step(k, _):
         @pl.when(k == 0)
         def _():
-            joined(1, 1)
-            gb(2).wait_recv()
-
-        @pl.when(k == 1)
-        def _():
             joined(1, 3)
             gb(0).wait_recv()
 
-        @pl.when(k == 2)
-        def _():
-            for part in range(HALF // 256):
-                ig(part).start()
-
-        @pl.when(k == 3)
+        for part in range(1, ITEMS // PART):
+
+            @pl.when(k == part)
+            def _():
+                for i in range((part - 1) * PART // 256, part * PART // 256):
+                    ig(i).start()
+
+        @pl.when(k == joined_at - 1)
+        def _():
+            joined(1, 2)
+
+        @pl.when(k == joined_at)
         def _():
             along_x(0)
 
-        off = pick(k % len(LAST), LAST)
-        first = pl.multiple_of((k // len(LAST)) * HALF, HALF)
-        q, ids = column(1, off)
-        here = pl.ds(first, HALF)
-        grads, losses = compute_tile(q, ids, items_ref[here], w * ITEMS + first, ig_total.at[here])
-        for cc in range(NC):
-            whose = lax.rem(core + cc, NC)
-            part = grads[cc * COL : (cc + 1) * COL]
-            rows = loss_rows(losses, cc)
-
-            @pl.when(k < len(LAST))
-            def _():
-                for s in range(2):
-                    tiles[whose, 1, off, s, 0:COL] = part[:, s * 128 : (s + 1) * 128]
-                tiles[whose, 1, off, 0, COL:TCOL] = rows
-                tiles[whose, 1, off, 1, COL:TCOL] = jnp.zeros((8, 128), jnp.float32)
-
-            @pl.when(k >= len(LAST))
-            def _():
-                for s in range(2):
-                    tiles[whose, 1, off, s, 0:COL] += part[:, s * 128 : (s + 1) * 128]
-                tiles[whose, 1, off, 0, COL:TCOL] += rows
-
-        @pl.when(k >= len(LAST))
-        def _():
-            tc(1, off).start()
+        first = pl.multiple_of(k * PART, PART)
+        here = pl.ds(first, PART)
+        pairs = [column(1, off) for off in LAST]
+        q = jnp.concatenate([p[0] for p in pairs], axis=0)
+        grads, losses = compute_tile(
+            q, [p[1] for p in pairs], items_ref[here], w * ITEMS + first, ig_total.at[here]
+        )
+        for n, off in enumerate(LAST):
+            for cc in range(NC):
+                whose = lax.rem(core + cc, NC)
+                at_row = (n * NC + cc) * COL
+                part = grads[at_row : at_row + COL]
+                rows = loss_rows(losses, n * NC + cc)
+
+                @pl.when(k == 0)
+                def _():
+                    for s in range(2):
+                        tiles[whose, 1, off, s, 0:COL] = part[:, s * 128 : (s + 1) * 128]
+                    tiles[whose, 1, off, 0, COL:TCOL] = rows
+                    tiles[whose, 1, off, 1, COL:TCOL] = jnp.zeros((8, 128), jnp.float32)
+
+                @pl.when(k > 0)
+                def _():
+                    for s in range(2):
+                        tiles[whose, 1, off, s, 0:COL] += part[:, s * 128 : (s + 1) * 128]
+                    tiles[whose, 1, off, 0, COL:TCOL] += rows
 
         return 0
 
-    lax.fori_loop(0, 2 * len(LAST), late_step, 0)
-
-    for k in range(HALF // 256, ITEMS // 256):
+    lax.fori_loop(0, ITEMS // PART, late_step, 0)
+
+    for off in LAST:
+        tc(1, off).start()
+    for k in range((ITEMS - PART) // 256, ITEMS // 256):
         ig(k).start()
     keep = pltpu.make_async_copy(ig_total, ig_own, out_s)
     keep.start()
-    joined(1, 2)
 
     def along_z(h, s):
         rows = slice(0, ZROWS if s == 0 else BLOCK)

time: 67.1 us -> 66.9 us (level)
  no operation moved by 1% of the time
where the time goes in v4:
time: 66.9 us; the launch traced here: 65.9 us
  Pallas kernels  65.2 us (97%)
    pallas_call x1, Pallas kernels, body(): pl.pallas_call(kernel, out_shape=small + (large, large), in_specs=[vmem]...  62.8 us
    pallas_call x1, Pallas kernels, body(): pl.pallas_call(finish, grid=(parts,), out_shape=small + (large,), in_spec...  2.43 us

profile of v4, /device:TPU:18, one launch (start us, length us, event | category | flops | bytes accessed | tf_op | source)
XLA Modules:
  0.0 65.9 jit_solution(3267316260818412484)
XLA Ops:
  0.6 62.8 %shard_map.58 = (f32[32,256]{1,0:T(8,128)}, f32[1,32]{1,0:T(1,128)}, f32[1024,256]{1,0:T(8,128)}, f32[1024,256]{1,0:T(8,128)}) custom-call(bf16[32,256]{1,0:T(8,128)(2,1)} %q_ref.1, s32[1,32]{1,0:T(1,128)} %bitcast.2, bf16[1024,256]{1,0:T(8,128)(2,1)} %items_ref.1), custom_call_target="tpu_custom_call" | custom-call | tf_op jit(solution)/shard_map/pallas_call | solution.py:410
  63.5 2.4 %shard_map.59 = (f32[32,256]{1,0:T(8,128)}, f32[1,32]{1,0:T(1,128)}, f32[1024,256]{1,0:T(8,128)}) custom-call(f32[32,256]{1,0:T(8,128)} %get-tuple-element.10.qgrad_in, f32[1,32]{1,0:T(1,128)} %get-tuple-element.11.loss_in, f32[1024,256]{1,0:T(8,128)} %get-tuple-element.12.own, f32[1024,256]{1,0:T(8,128)} %get-tuple-element.13.other), custom_call_target="tpu_custom_call" | custom-call | tf_op jit(solution)/shard_map/pallas_call | solution.py:442

commit v5 on v3

--- a/solution.py
+++ b/solution.py
@@ -43,12 +43,13 @@
     for c in range(panel.shape[0] // 128):
         scores = z[:, c * 128 : (c + 1) * 128] + logit_shift
         hit = place == c * 128
-        v = jnp.where(hit, -scores, scores)
-        e = jnp.exp2(jnp.abs(v) * (-log2e))
+        sign = jnp.where(hit, -1.0, 1.0)
+        v = scores * sign
+        e = jnp.exp2(jnp.abs(scores) * (-log2e))
         u = 1.0 + e
         r = 1.0 / u
         g = jnp.where(v >= 0, r, e * r)
-        slopes.append(jnp.where(hit, -g, g).astype(jnp.bfloat16))
+        slopes.append((g * sign).astype(jnp.bfloat16))
         relu = jnp.maximum(v, 0.0)
         product = e if product is None else product * u + e
         relus = relu if relus is None else relus + relu
@@ -326,11 +327,11 @@
 
     lax.fori_loop(0, 2 * len(LAST), late_step, 0)
 
+    joined(1, 2)
     for k in range(HALF // 256, ITEMS // 256):
         ig(k).start()
     keep = pltpu.make_async_copy(ig_total, ig_own, out_s)
     keep.start()
-    joined(1, 2)
 
     def along_z(h, s):
         rows = slice(0, ZROWS if s == 0 else BLOCK)

time: 67.1 us -> 67 us (level)
  no operation moved by 1% of the time
where the time goes in v5:
time: 67 us; the launch traced here: 65.9 us
  Pallas kernels  65.2 us (97%)
    pallas_call x1, Pallas kernels, body(): pl.pallas_call(kernel, out_shape=small + (large, large), in_specs=[vmem]...  62.8 us
    pallas_call x1, Pallas kernels, body(): pl.pallas_call(finish, grid=(parts,), out_shape=small + (large,), in_spec...  2.43 us

profile of v5, /device:TPU:18, one launch (start us, length us, event | category | flops | bytes accessed | tf_op | source)
XLA Modules:
  0.0 65.9 jit_solution(16752278946205009800)
XLA Ops:
  0.6 62.8 %shard_map.58 = (f32[32,256]{1,0:T(8,128)}, f32[1,32]{1,0:T(1,128)}, f32[1024,256]{1,0:T(8,128)}, f32[1024,256]{1,0:T(8,128)}) custom-call(bf16[32,256]{1,0:T(8,128)(2,1)} %q_ref.1, s32[1,32]{1,0:T(1,128)} %bitcast.2, bf16[1024,256]{1,0:T(8,128)(2,1)} %items_ref.1), custom_call_target="tpu_custom_call" | custom-call | tf_op jit(solution)/shard_map/pallas_call | solution.py:401
  63.5 2.4 %shard_map.59 = (f32[32,256]{1,0:T(8,128)}, f32[1,32]{1,0:T(1,128)}, f32[1024,256]{1,0:T(8,128)}) custom-call(f32[32,256]{1,0:T(8,128)} %get-tuple-element.10.qgrad_in, f32[1,32]{1,0:T(1,128)} %get-tuple-element.11.loss_in, f32[1024,256]{1,0:T(8,128)} %get-tuple-element.12.own, f32[1024,256]{1,0:T(8,128)} %get-tuple-element.13.other), custom_call_target="tpu_custom_call" | custom-call | tf_op jit(solution)/shard_map/pallas_call | solution.py:433
